TPU v7x, 1024 devices: a whole 4x8x16 slice. The times are simulated.
1024 devices in a mesh: expert: 8 (over y_hi, core), ffn: 16 (over z), dp: 8 (over x, y_lo).
Axes of the slice: x: 4, y: 8 (y_hi: 4, y_lo: 2; y = y_hi * 2 + y_lo), z: 16, core: 2. Of those that a mesh axis runs over, the one named last changes fastest.
Arguments:
- tokens: bfloat16 [768, 5120], P('expert', 'ffn'), may hold values from -6 to 6
- cotangent: bfloat16 [768, 5120], P('expert', 'ffn'), may hold values from -1.5 to 1.5
- routing: int32 [768, 1], P('expert'), may hold values from 0 to 7; in each aligned block of 96 rows (0 to 95, 96 to 191, ...) at most 24 rows name the same one
- gate_value: float32 [768], P('expert'), may hold values from 0.1 to 0.95
- expert_gate: bfloat16 [8, 5120, 8192], P('expert', 'ffn', 'dp'), may hold values from -0.078125 to 0.078125
- expert_up: bfloat16 [8, 5120, 8192], P('expert', 'ffn', 'dp'), may hold values from -0.078125 to 0.078125
- expert_down: bfloat16 [8, 8192, 5120], P('expert', 'dp', 'ffn'), may hold values from -0.0625 to 0.0625
- shared_gate: bfloat16 [5120, 8192], P('ffn', 'dp'), may hold values from -0.078125 to 0.078125
- shared_up: bfloat16 [5120, 8192], P('ffn', 'dp'), may hold values from -0.078125 to 0.078125
- shared_down: bfloat16 [8192, 5120], P('dp', 'ffn'), may hold values from -0.0625 to 0.0625
Outputs:
- layer_output: bfloat16 [768, 5120], P(('expert', 'dp'), 'ffn')
- grad_tokens: bfloat16 [768, 5120], P(('expert', 'dp'), 'ffn')
- grad_gate: bfloat16 [8, 5120, 8192], P('expert', 'ffn', 'dp')
- grad_up: bfloat16 [8, 5120, 8192], P('expert', 'ffn', 'dp')
Inputs may be any that keep to these rules, and one draw needn't show every extreme that they name: `routing`: in each source block of 96 tokens at most 24 tokens share a routed expert, and some block reaches 24.
All inputs are finite; a program needn't handle non-finite values.
Results may differ from a plain program's by a relative error of at most 0.0058.
Values may be sent and summed in bfloat16 or wider, within the bound.
A program may use at most 32 MiB of HBM per device.

v0:
```python
import jax
import jax.numpy as jnp
from jax import lax
from jax.sharding import PartitionSpec as P


def shortened(array):

    def short(part):
        return part.astype(jnp.bfloat16) if part.dtype == jnp.float32 else part

    return jax.tree.map(short, array)


def contract_last(operand, weights):
    return lax.dot_general(
        operand, weights, (((1,), (1,)), ((), ())), preferred_element_type=jnp.float32
    )


def contract_first(operand, weights):
    return lax.dot_general(
        operand, weights, (((0,), (0,)), ((), ())), preferred_element_type=jnp.float32
    )


def expert_rows(values):
    return jax.tree.map(
        lambda part, own: part.astype(own.dtype),
        lax.all_to_all(shortened(values), "expert", split_axis=0, concat_axis=0, tiled=True),
        values,
    )


def row_shares(values):
    return lax.psum_scatter(values, "ffn", scatter_dimension=0, tiled=True)


def row_gather(values):
    return (
        lax.all_gather(values[0], "ffn", axis=0, tiled=True),
        lax.all_gather(values[1], "ffn", axis=0, tiled=True),
    )


def token_total(values):
    return lax.psum_scatter(values, "dp", scatter_dimension=0, tiled=True)


def per_device(
    tokens,
    cotangent,
    routing,
    gate_value,
    expert_gate,
    expert_up,
    expert_down,
    shared_gate,
    shared_up,
    shared_down,
):
    experts = lax.axis_size("expert")
    tok_rows = tokens.shape[0]
    capacity = 2 * tok_rows // experts
    slot_count = experts * capacity
    chosen = routing[:, 0]
    onehot = (chosen[:, None] == jnp.arange(experts, dtype=jnp.int32)[None, :]).astype(jnp.int32)
    earlier = jnp.cumsum(onehot, axis=0) - onehot
    target = chosen * capacity + jnp.sum(earlier * onehot, axis=1)
    placing = (jnp.arange(slot_count, dtype=jnp.int32)[:, None] == target[None, :]).astype(
        jnp.bfloat16
    )
    scaled = (gate_value[:, None] * cotangent.astype(jnp.float32)).astype(jnp.bfloat16)
    outgoing = jnp.dot(placing, tokens, preferred_element_type=jnp.float32).astype(jnp.bfloat16)
    outgoing_cot = jnp.dot(placing, scaled, preferred_element_type=jnp.float32).astype(jnp.bfloat16)
    routed_in, routed_cot = expert_rows((outgoing, outgoing_cot))
    share_rows = (slot_count + tok_rows) // lax.axis_size("ffn")
    gate_part = jnp.concatenate(
        [
            jnp.dot(routed_in, expert_gate[0], preferred_element_type=jnp.float32),
            jnp.dot(tokens, shared_gate, preferred_element_type=jnp.float32),
        ],
        axis=0,
    )
    up_part = jnp.concatenate(
        [
            jnp.dot(routed_in, expert_up[0], preferred_element_type=jnp.float32),
            jnp.dot(tokens, shared_up, preferred_element_type=jnp.float32),
        ],
        axis=0,
    )
    grad_part = jnp.concatenate(
        [contract_last(routed_cot, expert_down[0]), contract_last(cotangent, shared_down)], axis=0
    )
    hidden = None
    gate_full, up_full = lax.psum((gate_part, up_part), "ffn")
    hidden = (gate_full * jax.nn.sigmoid(gate_full) * up_full).astype(jnp.bfloat16)
    offset_rows = lax.axis_index("ffn") * share_rows
    gate_share = lax.dynamic_slice_in_dim(gate_full, offset_rows, share_rows, 0)
    up_share = lax.dynamic_slice_in_dim(up_full, offset_rows, share_rows, 0)
    grad_share = row_shares(grad_part)
    squash = jax.nn.sigmoid(gate_share)
    grad_gate_h = (grad_share * up_share * squash * (1.0 + gate_share * (1.0 - squash))).astype(
        jnp.bfloat16
    )
    grad_up_h = (grad_share * (gate_share * squash)).astype(jnp.bfloat16)
    routed_out = jnp.dot(
        hidden[:slot_count], expert_down[0], preferred_element_type=jnp.float32
    ).astype(jnp.bfloat16)
    shared_out = jnp.dot(hidden[slot_count:], shared_down, preferred_element_type=jnp.float32)
    returned = expert_rows(routed_out)
    output_term = gate_value[:, None] * contract_first(placing, returned) + shared_out
    layer_output = token_total(output_term).astype(jnp.bfloat16)
    gate_rows, up_rows = row_gather((grad_gate_h, grad_up_h))
    routed_back = (
        contract_last(gate_rows[:slot_count], expert_gate[0])
        + contract_last(up_rows[:slot_count], expert_up[0])
    ).astype(jnp.bfloat16)
    came_back = expert_rows(routed_back)
    token_term = (
        contract_first(placing, came_back)
        + contract_last(gate_rows[slot_count:], shared_gate)
        + contract_last(up_rows[slot_count:], shared_up)
    )
    grad_tokens = token_total(token_term).astype(jnp.bfloat16)
    grad_gate = contract_first(routed_in, gate_rows[:slot_count]).astype(jnp.bfloat16)[None]
    grad_up = contract_first(routed_in, up_rows[:slot_count]).astype(jnp.bfloat16)[None]
    return (layer_output, grad_tokens, grad_gate, grad_up)


def solution(mesh):
    placed = (
        P("expert", "ffn"),
        P("expert", "ffn"),
        P("expert", None),
        P("expert"),
        P("expert", "ffn", "dp"),
        P("expert", "ffn", "dp"),
        P("expert", "dp", "ffn"),
        P("ffn", "dp"),
        P("ffn", "dp"),
        P("dp", "ffn"),
    )
    return jax.shard_map(
        per_device,
        mesh=mesh,
        in_specs=placed,
        out_specs=(
            P(("expert", "dp"), "ffn"),
            P(("expert", "dp"), "ffn"),
            P("expert", "ffn", "dp"),
            P("expert", "ffn", "dp"),
        ),
        check_vma=False,
    )
```

profile of v0, /device:TPU:8, one launch (start us, length us, event | category | flops | bytes accessed | tf_op | source)
XLA Modules:
  0.0 341.5 jit_solution(1526630885214670157)
XLA Ops:
  7.2 0.0 copy-start
  7.2 0.0 copy-start.10
  7.2 0.0 copy-start.5
  7.2 0.8 fusion.30
  8.0 0.1 reduce_window_sum.11
  8.2 0.8 select_reduce_fusion
  9.0 0.7 multiply_add_fusion
  9.7 1.7 convolution_convert_fusion.4
  11.4 6.2 %all-to-all-start = ((bf16[8,24,320]{2,1,0:T(8,128)(2,1)}), bf16[8,24,320]{2,1,0:T(8,128)(2,1)S(1)}, u32[]{:S(2)}, u32[]{:S(2)}) async-start(bf16[8,24,320]{2,1,0:T(8,128)(2,1)} %bitcast.1), calls=%async_computation | async-start | bytes 294912 | tf_op jit(solution)/shard_map/all_to_all | solution.py:30
  17.6 0.0 all-reduce.10.cloned.1.call-start
  17.7 1.4 fusion.34
  19.1 0.0 copy-start.1
  19.1 1.0 fusion.35
  20.1 7.0 %all-to-all-done = bf16[8,24,320]{2,1,0:T(8,128)(2,1)S(1)} async-done(((bf16[8,24,320]{2,1,0:T(8,128)(2,1)}), bf16[8,24,320]{2,1,0:T(8,128)(2,1)S(1)}, u32[]{:S(2)}, u32[]{:S(2)}) %all-to-all-start) | async-done | bytes 122912 | tf_op jit(solution)/shard_map/all_to_all | solution.py:30
  27.1 0.4 fusion.14
  27.5 0.4 fusion.10
  27.9 0.6 copy-done.7
  28.5 1.6 pad_maximum_fusion
  30.1 0.0 all-reduce.10.cloned.1.call-update
  30.1 0.9 copy-done.13
  31.0 0.9 convolution_convert_fusion.3
  31.9 3.4 all-to-all-start.2
  35.3 1.0 fusion.36
  36.3 8.4 %all-to-all-done.2 = bf16[8,24,320]{2,1,0:T(8,128)(2,1)S(1)} async-done(((bf16[8,24,320]{2,1,0:T(8,128)(2,1)}), bf16[8,24,320]{2,1,0:T(8,128)(2,1)S(1)}, u32[]{:S(2)}, u32[]{:S(2)}) %all-to-all-start.2) | async-done | bytes 122912 | tf_op jit(solution)/shard_map/all_to_all | solution.py:30
  44.7 0.4 fusion.6
  45.1 0.1 pad_maximum_fusion.2
  45.2 58.2 %fusion.1 = f32[24,1024]{1,0:T(8,128)S(1)} fusion(f32[288,1024]{1,0:T(8,128)S(1)} %pad_maximum_fusion.2), kind=kCustom, calls=%all-reduce-scatter.1 | all-reduce-scatter fusion | flops 393217 | bytes 1282048
  103.4 1.3 collective-permute-start.4
  104.7 3.9 %collective-permute-start.3 = (f32[24,1024]{1,0:T(8,128)S(1)}, f32[24,1024]{1,0:T(8,128)S(1)}, u32[]{:S(2)}, u32[]{:S(2)}) collective-permute-start(f32[24,1024]{1,0:T(8,128)S(1)} %fusion.1), channel_id=1, source_target_pairs={{0,16},{8,24},{16,32},{24,40},{32,48},{40,56},{48,64},{56,72},{64,... | collective-permute-start | bytes 294920
  108.6 3.2 collective-permute-start.2
  111.8 7.1 %collective-permute-start.5 = (f32[18,1024]{1,0:T(8,128)S(1)}, f32[18,1024]{1,0:T(8,128)S(1)}, u32[]{:S(2)}, u32[]{:S(2)}) collective-permute-start(f32[18,1024]{1,0:T(8,128)S(1)} %slice.33), channel_id=1, source_target_pairs={{0,32},{8,40},{16,48},{24,56},{32,64},{40,72},{48,80},{56,88},{64,... | collective-permute-start | bytes 221192
  118.8 1.3 dynamic-slice.12
  120.1 1.3 dynamic-slice.8
  122.7 0.6 concatenate.13
  123.4 74.7 %all-reduce.10.cloned.1.call-done = (f32[288,1024]{1,0:T(8,128)}, f32[288,1024]{1,0:T(8,128)}) async-done(((f32[288,1024]{1,0:T(8,128)}, f32[288,1024]{1,0:T(8,128)}), (f32[288,1024]{1,0:T(8,128)}, f32[288,1024]{1,0:T(8,128)})) %all-reduce.10.cloned.1.call-update) | async-done | bytes 2359312 | tf_op jit(solution)/shard_map/psum | solution.py:96
  198.0 2.0 multiply_convert_fusion
  200.0 1.3 fusion.31
  201.3 32.5 %all-gather = bf16[16,18,1024]{2,1,0:T(8,128)(2,1)S(1)} all-gather(bf16[1,18,1024]{2,1,0:T(8,128)(2,1)S(1)} %get-tuple-element.11), channel_id=1, replica_groups=mesh['expert'=8,'ffn'=16,'dp'=8] {'ffn'}, dimensions={0}, use_global_device_ids=true | all-gather | bytes 626688 | tf_op jit(solution)/shard_map/all_gather | solution.py:41
  233.8 0.2 reshape.26
  234.0 1.1 fusion.12
  235.1 1.2 fusion.3
  236.3 1.1 convolution_convert_fusion.2
  237.4 5.8 %all-to-all-start.1 = ((bf16[8,24,320]{2,1,0:T(8,128)(2,1)}), bf16[8,24,320]{2,1,0:T(8,128)(2,1)}, u32[]{:S(2)}, u32[]{:S(2)}) async-start(bf16[8,24,320]{2,1,0:T(8,128)(2,1)} %bitcast.6), calls=%async_computation.1 | async-start | bytes 294912 | tf_op jit(solution)/shard_map/all_to_all | solution.py:30
  243.3 30.8 %all-gather.1 = bf16[16,18,1024]{2,1,0:T(8,128)(2,1)S(1)} all-gather(bf16[1,18,1024]{2,1,0:T(8,128)(2,1)S(1)} %get-tuple-element.10), channel_id=1, replica_groups=mesh['expert'=8,'ffn'=16,'dp'=8] {'ffn'}, dimensions={0}, use_global_device_ids=true | all-gather | bytes 626688 | tf_op jit(solution)/shard_map/all_gather | solution.py:42
  274.1 0.2 reshape.28
  274.3 2.1 fusion.5
  276.4 6.9 %all-to-all-start.3 = ((bf16[8,24,320]{2,1,0:T(8,128)(2,1)}), bf16[8,24,320]{2,1,0:T(8,128)(2,1)}, u32[]{:S(2)}, u32[]{:S(2)}) async-start(bf16[8,24,320]{2,1,0:T(8,128)(2,1)} %bitcast.12), calls=%async_computation.3 | async-start | bytes 294912 | tf_op jit(solution)/shard_map/all_to_all | solution.py:30
  283.4 1.1 convolution_multiply_fusion
  284.5 1.3 convolution_add_fusion.3
  285.8 7.9 %all-to-all-done.3 = bf16[8,24,320]{2,1,0:T(8,128)(2,1)} async-done(((bf16[8,24,320]{2,1,0:T(8,128)(2,1)}), bf16[8,24,320]{2,1,0:T(8,128)(2,1)}, u32[]{:S(2)}, u32[]{:S(2)}) %all-to-all-start.3) | async-done | bytes 122912 | tf_op jit(solution)/shard_map/all_to_all | solution.py:30
  293.8 1.1 fusion.24
  294.9 0.4 convolution_add_fusion.2
  295.3 0.4 convolution_add_fusion.1
  295.6 20.2 %fusion.33 = (f32[16,320]{1,0:T(8,128)S(1)}, f32[16,320]{1,0:T(8,128)S(1)}) fusion(f32[96,320]{1,0:T(8,128)S(1)} %convolution_add_fusion.3, f32[96,320]{1,0:T(8,128)S(1)} %convolution_add_fusion.1), kind=kCustom, calls=%all-reduce-scatter.3 | all-reduce-scatter fusion | flops 81921 | bytes 290816
  315.9 1.9 collective-permute-start.1
  317.8 4.9 %collective-permute-start = (bf16[16,320]{1,0:T(8,128)(2,1)S(1)}, bf16[16,320]{1,0:T(8,128)(2,1)S(1)}, u32[]{:S(2)}, u32[]{:S(2)}) collective-permute-start(bf16[16,320]{1,0:T(8,128)(2,1)S(1)} %convert), channel_id=1, source_target_pairs={{0,1},{1,2},{2,3},{3,4},{4,5},{5,6},{6,7},{8,9},{9,10},{10,11},{11... | collective-permute-start | bytes 30728
  322.7 1.2 fusion.4
  324.0 4.1 %collective-permute-start.7 = (bf16[12,320]{1,0:T(8,128)(2,1)S(1)}, bf16[12,320]{1,0:T(8,128)(2,1)S(1)}, u32[]{:S(2)}, u32[]{:S(2)}) collective-permute-start(bf16[12,320]{1,0:T(8,128)(2,1)S(1)} %slice.34), channel_id=1, source_target_pairs={{0,2},{1,3},{2,4},{3,5},{4,6},{5,7},{8,10},{9,11},{10,12},{11,13},... | collective-permute-start | bytes 23048
  328.1 2.2 collective-permute-start.6
  330.4 0.3 concatenate.12
  330.7 0.6 dynamic-slice_convert_fusion.1
  331.3 2.4 collective-permute-done.6
  333.7 0.3 concatenate.14
  334.0 0.6 dynamic-slice_convert_fusion
  (37 shorter events, 0.1 us)
Async XLA Ops:
  7.2 20.0 %copy-start = (bf16[1,320,1024]{2,1,0:T(8,128)(2,1)S(1)}, bf16[1,320,1024]{2,1,0:T(8,128)(2,1)}, u32[]{:S(2)}) copy-start(bf16[1,320,1024]{2,1,0:T(8,128)(2,1)} %param.14) | copy-start | bytes 1966084
  7.2 11.9 %copy-start.10 = (bf16[96,320]{1,0:T(8,128)(2,1)S(1)}, bf16[96,320]{1,0:T(8,128)(2,1)}, u32[]{:S(2)}) copy-start(bf16[96,320]{1,0:T(8,128)(2,1)} %param.10) | copy-start | bytes 184324
  7.2 11.9 %copy-start.5 = (bf16[320,1024]{1,0:T(8,128)(2,1)S(1)}, bf16[320,1024]{1,0:T(8,128)(2,1)}, u32[]{:S(2)}) copy-start(bf16[320,1024]{1,0:T(8,128)(2,1)} %param.18) | copy-start | bytes 1966084
  11.4 15.7 %all-to-all-start = ((bf16[8,24,320]{2,1,0:T(8,128)(2,1)}), bf16[8,24,320]{2,1,0:T(8,128)(2,1)S(1)}, u32[]{:S(2)}, u32[]{:S(2)}) async-start(bf16[8,24,320]{2,1,0:T(8,128)(2,1)} %bitcast.1), calls=%async_computation | async-start | bytes 294912 | tf_op jit(solution)/shard_map/all_to_all | solution.py:30
  17.6 180.4 %all-reduce.10.cloned.1.call-start = ((), (), s32[]{:S(2)}) async-start(), calls=%async_computation.4 | async-start | bytes 4718592 | tf_op jit(solution)/shard_map/psum | solution.py:96
  19.1 8.4 %copy-start.1 = (bf16[1,320,1024]{2,1,0:T(8,128)(2,1)S(1)}, bf16[1,320,1024]{2,1,0:T(8,128)(2,1)}, u32[]{:S(2)}) copy-start(bf16[1,320,1024]{2,1,0:T(8,128)(2,1)} %param.15) | copy-start | bytes 1966084
  27.5 1.0 copy-start.7
  30.1 0.9 copy-start.13
  30.1 0.9 copy-start.14
  30.1 5.2 %copy-start.2 = (bf16[1024,320]{0,1:T(8,128)(2,1)S(1)}, bf16[1024,320]{0,1:T(8,128)(2,1)}, u32[]{:S(2)}) copy-start(bf16[1024,320]{0,1:T(8,128)(2,1)} %param.19) | copy-start | bytes 1966084
  31.0 13.7 %copy-start.11 = (bf16[1,1024,320]{1,2,0:T(8,128)(2,1)S(1)}, bf16[1,1024,320]{1,2,0:T(8,128)(2,1)}, u32[]{:S(2)}) copy-start(bf16[1,1024,320]{1,2,0:T(8,128)(2,1)} %param.16) | copy-start | bytes 1966084
  31.9 12.8 %all-to-all-start.2 = ((bf16[8,24,320]{2,1,0:T(8,128)(2,1)}), bf16[8,24,320]{2,1,0:T(8,128)(2,1)S(1)}, u32[]{:S(2)}, u32[]{:S(2)}) async-start(bf16[8,24,320]{2,1,0:T(8,128)(2,1)} %bitcast.8), calls=%async_computation.2 | async-start | bytes 294912 | tf_op jit(solution)/shard_map/all_to_all | solution.py:30
  36.3 8.8 %copy-start.8 = (f32[96,1024]{1,0:T(8,128)S(1)}, f32[96,1024]{1,0:T(8,128)}, u32[]{:S(2)}) copy-start(f32[96,1024]{1,0:T(8,128)} %fusion.36) | copy-start | bytes 1179652
  103.4 19.3 %collective-permute-start.4 = (f32[24,1024]{1,0:T(8,128)S(1)}, f32[24,1024]{1,0:T(8,128)S(1)}, u32[]{:S(2)}, u32[]{:S(2)}) collective-permute-start(f32[24,1024]{1,0:T(8,128)S(1)} %fusion.1), channel_id=1, source_target_pairs={{0,24},{8,32},{16,40},{24,48},{32,56},{40,64},{48,72},{56,80},{64,... | collective-permute-start | bytes 294920
  104.7 18.0 %collective-permute-start.3 = (f32[24,1024]{1,0:T(8,128)S(1)}, f32[24,1024]{1,0:T(8,128)S(1)}, u32[]{:S(2)}, u32[]{:S(2)}) collective-permute-start(f32[24,1024]{1,0:T(8,128)S(1)} %fusion.1), channel_id=1, source_target_pairs={{0,16},{8,24},{16,32},{24,40},{32,48},{40,56},{48,64},{56,72},{64,... | collective-permute-start | bytes 294920
  108.6 14.1 %collective-permute-start.2 = (f32[24,1024]{1,0:T(8,128)S(1)}, f32[24,1024]{1,0:T(8,128)S(1)}, u32[]{:S(2)}, u32[]{:S(2)}) collective-permute-start(f32[24,1024]{1,0:T(8,128)S(1)} %fusion.1), channel_id=1, source_target_pairs={{0,8},{8,16},{16,24},{24,32},{32,40},{40,48},{48,56},{56,64},{64,7... | collective-permute-start | bytes 294920
  111.8 10.9 %collective-permute-start.5 = (f32[18,1024]{1,0:T(8,128)S(1)}, f32[18,1024]{1,0:T(8,128)S(1)}, u32[]{:S(2)}, u32[]{:S(2)}) collective-permute-start(f32[18,1024]{1,0:T(8,128)S(1)} %slice.33), channel_id=1, source_target_pairs={{0,32},{8,40},{16,48},{24,56},{32,64},{40,72},{48,80},{56,88},{64,... | collective-permute-start | bytes 221192
  200.0 36.3 %copy-start.9 = (bf16[288,1024]{1,0:T(8,128)(2,1)}, bf16[288,1024]{1,0:T(8,128)(2,1)S(1)}, u32[]{:S(2)}) copy-start(bf16[288,1024]{1,0:T(8,128)(2,1)S(1)} %multiply_convert_fusion) | copy-start | bytes 1769476
  234.0 2.4 copy-start.12
  237.4 39.0 %all-to-all-start.1 = ((bf16[8,24,320]{2,1,0:T(8,128)(2,1)}), bf16[8,24,320]{2,1,0:T(8,128)(2,1)}, u32[]{:S(2)}, u32[]{:S(2)}) async-start(bf16[8,24,320]{2,1,0:T(8,128)(2,1)} %bitcast.6), calls=%async_computation.1 | async-start | bytes 294912 | tf_op jit(solution)/shard_map/all_to_all | solution.py:30
  274.3 10.2 %copy-start.3 = (bf16[1024,320]{0,1:T(8,128)(2,1)S(1)}, bf16[1024,320]{0,1:T(8,128)(2,1)}, u32[]{:S(2)}) copy-start(bf16[1024,320]{0,1:T(8,128)(2,1)} %param.19) | copy-start | bytes 1966084
  276.4 18.5 %copy-start.4 = (bf16[320,1024]{1,0:T(8,128)(2,1)S(1)}, bf16[320,1024]{1,0:T(8,128)(2,1)}, u32[]{:S(2)}) copy-start(bf16[320,1024]{1,0:T(8,128)(2,1)} %param.17) | copy-start | bytes 1966084
  276.4 17.3 %all-to-all-start.3 = ((bf16[8,24,320]{2,1,0:T(8,128)(2,1)}), bf16[8,24,320]{2,1,0:T(8,128)(2,1)}, u32[]{:S(2)}, u32[]{:S(2)}) async-start(bf16[8,24,320]{2,1,0:T(8,128)(2,1)} %bitcast.12), calls=%async_computation.3 | async-start | bytes 294912 | tf_op jit(solution)/shard_map/all_to_all | solution.py:30
  285.8 9.5 %copy-start.6 = (bf16[320,1024]{1,0:T(8,128)(2,1)S(1)}, bf16[320,1024]{1,0:T(8,128)(2,1)}, u32[]{:S(2)}) copy-start(bf16[320,1024]{1,0:T(8,128)(2,1)} %param.18) | copy-start | bytes 1966084
  315.9 14.5 %collective-permute-start.1 = (bf16[12,320]{1,0:T(8,128)(2,1)S(1)}, bf16[12,320]{1,0:T(8,128)(2,1)S(1)}, u32[]{:S(2)}, u32[]{:S(2)}) collective-permute-start(bf16[12,320]{1,0:T(8,128)(2,1)S(1)} %slice.32), channel_id=1, source_target_pairs={{0,2},{1,3},{2,4},{3,5},{4,6},{5,7},{8,10},{9,11},{10,12},{11,13},... | collective-permute-start | bytes 23048
  317.8 12.6 %collective-permute-start = (bf16[16,320]{1,0:T(8,128)(2,1)S(1)}, bf16[16,320]{1,0:T(8,128)(2,1)S(1)}, u32[]{:S(2)}, u32[]{:S(2)}) collective-permute-start(bf16[16,320]{1,0:T(8,128)(2,1)S(1)} %convert), channel_id=1, source_target_pairs={{0,1},{1,2},{2,3},{3,4},{4,5},{5,6},{6,7},{8,9},{9,10},{10,11},{11... | collective-permute-start | bytes 30728
  324.0 7.4 %collective-permute-start.7 = (bf16[12,320]{1,0:T(8,128)(2,1)S(1)}, bf16[12,320]{1,0:T(8,128)(2,1)S(1)}, u32[]{:S(2)}, u32[]{:S(2)}) collective-permute-start(bf16[12,320]{1,0:T(8,128)(2,1)S(1)} %slice.34), channel_id=1, source_target_pairs={{0,2},{1,3},{2,4},{3,5},{4,6},{5,7},{8,10},{9,11},{10,12},{11,13},... | collective-permute-start | bytes 23048
  328.1 5.6 %collective-permute-start.6 = (bf16[16,320]{1,0:T(8,128)(2,1)S(1)}, bf16[16,320]{1,0:T(8,128)(2,1)S(1)}, u32[]{:S(2)}, u32[]{:S(2)}) collective-permute-start(bf16[16,320]{1,0:T(8,128)(2,1)S(1)} %convert.1), channel_id=1, source_target_pairs={{0,1},{1,2},{2,3},{3,4},{4,5},{5,6},{6,7},{8,9},{9,10},{10,11},{11... | collective-permute-start | bytes 30728
Sparse Core Ops, SparseCore 0:
  30.2 167.7 all-reduce.9
where the time goes:
time: 343 us; the launch traced here: 341 us
  blocking collectives  142 us (41%)
  waiting for transfers between devices  100 us (29%)
  starting transfers between devices  51 us (15%)
  matrix products  18.2 us (5%)
  between operations  15.8 us (5%)
  other arithmetic  7.42 us (2%)
  local copies, waits for them, and re-layouts  6.97 us (2%)
    unnamed x2, blocking collectives  78.4 us
    psum x1, waiting for transfers between devices, per_device(): gate_full, up_full = lax.psum((gate_part, up_part), 'ffn')  74.7 us
    all_gather x1, blocking collectives, row_gather(): lax.all_gather(values[0], 'ffn', axis=0, tiled=True)  32.5 us
    all_gather x1, blocking collectives, row_gather(): lax.all_gather(values[1], 'ffn', axis=0, tiled=True)  30.8 us
    unnamed x8, starting transfers between devices  28.6 us
    all_to_all x4, waiting for transfers between devices, expert_rows(): lax.all_to_all(shortened(values), 'expert', split_axis=0, concat_axis=0,...  23.3 us
    all_to_all x4, starting transfers between devices, expert_rows(): lax.all_to_all(shortened(values), 'expert', split_axis=0, concat_axis=0,...  22.3 us
  transfers between devices with their start and end apart: 13, of which 5 were waited for; matrix products, arithmetic and copies ran while one was open for 21% of the time, Pallas kernels for 0%

commit v1 on v0

v1 whole, which is shorter than its diff:
```python
import functools

import jax
import jax.numpy as jnp
from jax import lax
from jax.experimental import pallas as pl
from jax.experimental.pallas import tpu as pltpu
from jax.sharding import PartitionSpec as P

MESH = pl.DeviceIdType.MESH
F32 = jnp.float32
BF16 = jnp.bfloat16

TOK = 96
CAP = 24
NE = 8
NF = 16
ND = 8
SLOTS = NE * CAP
WIDTH = 320
HID = 1024
SUB = 48
COL = 128
STREAMS = 3
HOPS = (8, 7)
NARROW = (6, 4)
WIDE = max(HOPS[0] - NARROW[0], HOPS[1] - NARROW[1])
ROWS_DP = TOK // ND


def dot(a, b):
    return lax.dot_general(a, b, (((1,), (0,)), ((), ())), preferred_element_type=F32)


def dot_last(a, b):
    return lax.dot_general(a, b, (((1,), (1,)), ((), ())), preferred_element_type=F32)


def dot_first(a, b):
    return lax.dot_general(a, b, (((0,), (0,)), ((), ())), preferred_element_type=F32)


def kernel(
    tok_hbm, cot_hbm, routing_hbm, gate_hbm, eg_hbm, eu_hbm, ed_hbm, sg_hbm, su_hbm, sd_hbm,
    lo_hbm, gt_hbm, gg_hbm, gu_hbm,
    tok, cot, routing, gate, eg, eu, ed, sg, su, sd,
    outbox, inbox, routed_in, routed_cot, part_s, part_r,
    stage_b, stage_f, held_b, held_f, act_s, act_r,
    outbox2, inbox2, term, outbox3, inbox3, lo, gt, gg, gu,
    load_sem, store_sem, rs_send, rs_recv, ag_send, ag_recv, x_send, x_recv, y_send, y_recv, z_send, z_recv,
):
    me_e, me_f, me_d = lax.axis_index("expert"), lax.axis_index("ffn"), lax.axis_index("dp")
    nbr = (lax.rem(me_f + 1, NF), lax.rem(me_f + NF - 1, NF))

    loads = [
        pltpu.make_async_copy(src, dst, load_sem.at[n])
        for n, (src, dst) in enumerate(
            [
                (routing_hbm, routing), (gate_hbm, gate), (tok_hbm, tok), (cot_hbm, cot),
                (sg_hbm, sg), (su_hbm, su), (sd_hbm, sd),
                (eg_hbm.at[0], eg), (eu_hbm.at[0], eu), (ed_hbm.at[0], ed),
            ]
        )
    ]
    for load in loads:
        load.start()

    barrier = pltpu.get_barrier_semaphore()
    for other in nbr:
        pl.semaphore_signal(barrier, inc=1, device_id={"ffn": other}, device_id_type=MESH)
    for k in range(1, NE):
        pl.semaphore_signal(
            barrier, inc=1, device_id={"expert": lax.rem(me_e + k, NE)}, device_id_type=MESH
        )
    for k in range(1, ND):
        pl.semaphore_signal(
            barrier, inc=1, device_id={"dp": lax.rem(me_d + k, ND)}, device_id_type=MESH
        )

    for n in range(4):
        loads[n].wait()
    chosen = routing[...]
    onehot = (chosen == lax.broadcasted_iota(jnp.int32, (TOK, NE), 1)).astype(F32)
    before = (
        lax.broadcasted_iota(jnp.int32, (TOK, TOK), 0) > lax.broadcasted_iota(jnp.int32, (TOK, TOK), 1)
    )
    earlier = dot(before.astype(BF16), onehot.astype(BF16))
    slot = jnp.sum(earlier * onehot, axis=1, keepdims=True).astype(jnp.int32)
    target = chosen * (2 * CAP) + slot
    boxes = lax.broadcasted_iota(jnp.int32, (TOK, 2 * SLOTS), 1)
    pick_first = (boxes == target).astype(BF16)
    pick_second = (boxes == target + CAP).astype(BF16)
    same = (
        lax.broadcasted_iota(jnp.int32, (TOK, TOK), 0) == lax.broadcasted_iota(jnp.int32, (TOK, TOK), 1)
    )
    gate_column = jnp.sum(
        jnp.where(same, jnp.broadcast_to(gate[...].reshape(1, TOK), (TOK, TOK)), 0.0), axis=1, keepdims=True
    )
    scaled = (gate_column * cot[...].astype(F32)).astype(BF16)
    outbox[...] = (dot_first(pick_first, tok[...]) + dot_first(pick_second, scaled)).astype(BF16)

    pl.semaphore_wait(barrier, 2 + (NE - 1) + (ND - 1))

    def box(ref, index):
        return ref.at[pl.ds(pl.multiple_of(index * 2 * CAP, 2 * CAP), 2 * CAP)]

    def exchange(source, target_ref, send, recv, k):
        peer = lax.rem(me_e + k, NE)
        return pltpu.make_async_remote_copy(
            src_ref=box(source, peer), dst_ref=box(target_ref, me_e),
            send_sem=send.at[k], recv_sem=recv.at[k],
            device_id={"expert": peer}, device_id_type=MESH,
        )

    def arrival(source, target_ref, send, recv, k):
        peer = lax.rem(me_e + NE - k, NE)
        return pltpu.make_async_remote_copy(
            src_ref=box(source, me_e), dst_ref=box(target_ref, peer),
            send_sem=send.at[k], recv_sem=recv.at[k],
            device_id={"expert": peer}, device_id_type=MESH,
        )

    for k in range(1, NE):
        exchange(outbox, inbox, x_send, x_recv, k).start()
    box(inbox, me_e)[...] = box(outbox, me_e)[...]

    for n in range(4, 7):
        loads[n].wait()
    part_s[0] = dot(tok[...], sg[...])
    part_s[1] = dot(tok[...], su[...])
    part_s[2] = dot_last(cot[...], sd[...])

    def block(ref, stream, owner):
        columns = pl.ds(pl.multiple_of(lax.div(owner, 2) * COL, COL), COL)
        half = lax.rem(owner, 2)
        if stream == 0:
            first = half * SUB
        else:
            first = half * 2 * SUB + (stream - 1) * SUB
        return ref.at[:, pl.ds(pl.multiple_of(first, SUB), SUB), columns]

    def mine(stream):
        return (part_s if stream == 0 else part_r), (act_s if stream == 0 else act_r)

    def slots(narrow, wide, stream, way, step):
        if step < NARROW[way]:
            return narrow.at[stream, way, step]
        return wide.at[stream, way, step - NARROW[way]]

    def sum_copy(stream, way, step):
        return pltpu.make_async_remote_copy(
            src_ref=slots(stage_b, stage_f, stream, way, step),
            dst_ref=slots(held_b, held_f, stream, way, step),
            send_sem=rs_send.at[stream, way, step], recv_sem=rs_recv.at[stream, way, step],
            device_id={"ffn": nbr[way]}, device_id_type=MESH,
        )

    def sum_step(stream, way, step):
        if way == 0:
            owner = lax.rem(me_f + HOPS[0] - step, NF)
        else:
            owner = lax.rem(me_f + NF - HOPS[1] + step, NF)
        value = block(mine(stream)[0], stream, owner)[...]
        if step > 0:
            sum_copy(stream, way, step - 1).wait_recv()
            value = value + slots(held_b, held_f, stream, way, step - 1)[...].astype(F32)
        stage = slots(stage_b, stage_f, stream, way, step)
        stage[...] = value.astype(stage.dtype)
        sum_copy(stream, way, step).start()

    def sum_end(stream):
        part, act = mine(stream)
        value = block(part, stream, me_f)[...]
        for way in range(2):
            last = HOPS[way] - 1
            sum_copy(stream, way, last).wait_recv()
            value = value + slots(held_b, held_f, stream, way, last)[...].astype(F32)
        g, u, p = value[0], value[1], value[2]
        squash = jax.nn.sigmoid(g)
        silu = g * squash
        own = block(act, stream, me_f)
        own[0] = (silu * u).astype(BF16)
        own[1] = (p * u * squash * (1.0 + g * (1.0 - squash))).astype(BF16)
        own[2] = (p * silu).astype(BF16)

    def gather_copy(stream, way, step, owner):
        ref = block(mine(stream)[1], stream, owner)
        return pltpu.make_async_remote_copy(
            src_ref=ref, dst_ref=ref,
            send_sem=ag_send.at[stream, way, step], recv_sem=ag_recv.at[stream, way, step],
            device_id={"ffn": nbr[way]}, device_id_type=MESH,
        )

    def gather_owner(way, step):
        return lax.rem(me_f + NF - step, NF) if way == 0 else lax.rem(me_f + step, NF)

    def gather_arrived(stream, way, step):
        gather_copy(stream, way, step, gather_owner(way, step + 1)).wait_recv()

    def gather_step(stream, way, step):
        if step > 0:
            gather_arrived(stream, way, step - 1)
        gather_copy(stream, way, step, gather_owner(way, step)).start()

    def gather_end(stream):
        for way in range(2):
            gather_arrived(stream, way, HOPS[way] - 1)

    def turn(stream, now):
        if now < 0:
            return
        if now < HOPS[0]:
            for way in range(2):
                if now < HOPS[way]:
                    sum_step(stream, way, now)
        elif now < 2 * HOPS[0]:
            if now == HOPS[0]:
                sum_end(stream)
            for way in range(2):
                if now - HOPS[0] < HOPS[way]:
                    gather_step(stream, way, now - HOPS[0])
        elif now == 2 * HOPS[0]:
            gather_end(stream)

    LEAD = 2
    for now in range(LEAD):
        turn(0, now)

    for k in range(1, NE):
        arrival(outbox, inbox, x_send, x_recv, k).wait_recv()
    came = inbox[...].astype(F32)
    routed_in[...] = jnp.concatenate(
        [came[2 * CAP * e : 2 * CAP * e + CAP] for e in range(NE)], axis=0
    ).astype(BF16)
    routed_cot[...] = jnp.concatenate(
        [came[2 * CAP * e + CAP : 2 * CAP * (e + 1)] for e in range(NE)], axis=0
    ).astype(BF16)
    for n in range(7, 10):
        loads[n].wait()
    part_r[0] = dot(routed_in[...], eg[...])
    part_r[1] = dot(routed_in[...], eu[...])
    part_r[2] = dot_last(routed_cot[...], ed[...])

    LAG = 4
    for now in range(LEAD, 2 * HOPS[0] + LEAD + LAG + 1):
        for stream in range(1, STREAMS):
            turn(stream, now - LEAD)
        if now < HOPS[0]:
            turn(0, now)
        else:
            late = now - (LEAD + LAG)
            if late >= HOPS[0]:
                turn(0, late)
        if now - LEAD == 2 * HOPS[0]:
            routed_out = dot(act_r[0], ed[...])
            routed_back = dot_last(act_r[1], eg[...]) + dot_last(act_r[2], eu[...])
            for e in range(NE):
                outbox2[2 * CAP * e : 2 * CAP * (e + 1)] = jnp.concatenate(
                    [routed_out[CAP * e : CAP * (e + 1)], routed_back[CAP * e : CAP * (e + 1)]], axis=0
                ).astype(BF16)
            for k in range(1, NE):
                exchange(outbox2, inbox2, y_send, y_recv, k).start()
            box(inbox2, me_e)[...] = box(outbox2, me_e)[...]

    shared_out = dot(act_s[0], sd[...])
    shared_back = dot_last(act_s[1], sg[...]) + dot_last(act_s[2], su[...])
    for k in range(1, NE):
        arrival(outbox2, inbox2, y_send, y_recv, k).wait_recv()
    term[0] = gate_column * dot(pick_first, inbox2[...]) + shared_out
    term[1] = dot(pick_second, inbox2[...]) + shared_back
    for d in range(ND):
        outbox3[d, :ROWS_DP] = term[0, ROWS_DP * d : ROWS_DP * (d + 1)]
        outbox3[d, ROWS_DP:] = term[1, ROWS_DP * d : ROWS_DP * (d + 1)]

    def dp_send(k):
        peer = lax.rem(me_d + k, ND)
        return pltpu.make_async_remote_copy(
            src_ref=outbox3.at[peer], dst_ref=inbox3.at[k],
            send_sem=z_send.at[k], recv_sem=z_recv.at[k],
            device_id={"dp": peer}, device_id_type=MESH,
        )

    for k in range(1, ND):
        dp_send(k).start()

    gg[...] = dot_first(routed_in[...], act_r[1]).astype(BF16)
    gu[...] = dot_first(routed_in[...], act_r[2]).astype(BF16)
    stores = [
        pltpu.make_async_copy(gg, gg_hbm.at[0], store_sem.at[0]),
        pltpu.make_async_copy(gu, gu_hbm.at[0], store_sem.at[1]),
    ]
    for store in stores:
        store.start()

    total = outbox3[me_d]
    for k in range(1, ND):
        dp_send(k).wait_recv()
        total = total + inbox3[k]
    lo[...] = total[:ROWS_DP].astype(BF16)
    gt[...] = total[ROWS_DP:].astype(BF16)
    last = [
        pltpu.make_async_copy(lo, lo_hbm, store_sem.at[2]),
        pltpu.make_async_copy(gt, gt_hbm, store_sem.at[3]),
    ]
    for store in last:
        store.start()
    for stream in range(STREAMS):
        for way in range(2):
            for step in range(HOPS[way]):
                sum_copy(stream, way, step).wait_send()
                gather_copy(stream, way, step, gather_owner(way, step)).wait_send()
    for k in range(1, NE):
        exchange(outbox, inbox, x_send, x_recv, k).wait_send()
        exchange(outbox2, inbox2, y_send, y_recv, k).wait_send()
    for k in range(1, ND):
        dp_send(k).wait_send()
    for store in stores + last:
        store.wait()


def per_device(*args):
    vmem = pltpu.VMEM
    dma = pltpu.SemaphoreType.DMA
    any_spec = pl.BlockSpec(memory_space=pl.ANY)
    return pl.pallas_call(
        kernel,
        out_shape=(
            jax.ShapeDtypeStruct((ROWS_DP, WIDTH), BF16),
            jax.ShapeDtypeStruct((ROWS_DP, WIDTH), BF16),
            jax.ShapeDtypeStruct((1, WIDTH, HID), BF16),
            jax.ShapeDtypeStruct((1, WIDTH, HID), BF16),
        ),
        in_specs=[any_spec] * 10,
        out_specs=(any_spec,) * 4,
        scratch_shapes=[
            vmem((TOK, WIDTH), BF16), vmem((TOK, WIDTH), BF16), vmem((TOK, 1), jnp.int32), vmem((TOK,), F32),
            vmem((WIDTH, HID), BF16), vmem((WIDTH, HID), BF16), vmem((HID, WIDTH), BF16),
            vmem((WIDTH, HID), BF16), vmem((WIDTH, HID), BF16), vmem((HID, WIDTH), BF16),
            vmem((2 * SLOTS, WIDTH), BF16), vmem((2 * SLOTS, WIDTH), BF16),
            vmem((SLOTS, WIDTH), BF16), vmem((SLOTS, WIDTH), BF16),
            vmem((3, TOK, HID), F32), vmem((3, SLOTS, HID), F32),
            vmem((STREAMS, 2, max(NARROW), 3, SUB, COL), BF16), vmem((STREAMS, 2, WIDE, 3, SUB, COL), F32),
            vmem((STREAMS, 2, max(NARROW), 3, SUB, COL), BF16), vmem((STREAMS, 2, WIDE, 3, SUB, COL), F32),
            vmem((3, TOK, HID), BF16), vmem((3, SLOTS, HID), BF16),
            vmem((2 * SLOTS, WIDTH), BF16), vmem((2 * SLOTS, WIDTH), BF16),
            vmem((2, TOK, WIDTH), F32),
            vmem((ND, 2 * ROWS_DP, WIDTH), F32), vmem((ND, 2 * ROWS_DP, WIDTH), F32),
            vmem((ROWS_DP, WIDTH), BF16), vmem((ROWS_DP, WIDTH), BF16),
            vmem((WIDTH, HID), BF16), vmem((WIDTH, HID), BF16),
            dma((10,)), dma((4,)),
            dma((STREAMS, 2, HOPS[0])), dma((STREAMS, 2, HOPS[0])),
            dma((STREAMS, 2, HOPS[0])), dma((STREAMS, 2, HOPS[0])),
            dma((NE,)), dma((NE,)), dma((NE,)), dma((NE,)), dma((ND,)), dma((ND,)),
        ],
        compiler_params=pltpu.CompilerParams(
            collective_id=0, has_side_effects=True, vmem_limit_bytes=48 * 1024 * 1024
        ),
    )(*args)


def solution(mesh):
    placed = (
        P("expert", "ffn"),
        P("expert", "ffn"),
        P("expert", None),
        P("expert"),
        P("expert", "ffn", "dp"),
        P("expert", "ffn", "dp"),
        P("expert", "dp", "ffn"),
        P("ffn", "dp"),
        P("ffn", "dp"),
        P("dp", "ffn"),
    )
    return jax.shard_map(
        per_device,
        mesh=mesh,
        in_specs=placed,
        out_specs=(
            P(("expert", "dp"), "ffn"),
            P(("expert", "dp"), "ffn"),
            P("expert", "ffn", "dp"),
            P("expert", "ffn", "dp"),
        ),
        check_vma=False,
    )
```

time: 343 us -> 122 us (0.36)
  the two profiles are of different devices: /device:TPU:8 before, /device:TPU:14 now
where the time goes in v1:
time: 122 us
  Pallas kernels  110 us (90%)
  local copies, waits for them, and re-layouts  11 us (9%)
    pallas_call x1, Pallas kernels, per_device(): pl.pallas_call(kernel, out_shape=(jax.ShapeDtypeStruct((ROWS_DP, WIDTH),...  110 us
    unnamed x23, local copies, waits for them, and re-layouts  11 us

profile of v1, /device:TPU:14, one launch (start us, length us, event | category | flops | bytes accessed | tf_op | source)
XLA Modules:
  0.0 121.6 jit_solution(242455154850096574)
XLA Ops:
  0.6 1.4 %copy.14.routing_hbm = s32[96,1]{1,0:T(8,128)} copy(s32[96,1]{0,1:T(1,128)} %param.12) | data formatting | bytes 768 | tf_op args[2]
  2.0 0.0 copy-start.2
  2.0 1.5 %copy.15.ed_hbm = bf16[1,1024,320]{2,1,0:T(8,128)(2,1)S(1)} copy(bf16[1,1024,320]{1,2,0:T(8,128)(2,1)} %param.16) | data formatting | bytes 1310720 | tf_op args[6]
  3.5 0.0 copy-start
  3.5 0.0 copy-start.1
  3.5 0.0 copy-start.7
  3.6 1.5 %copy.16.sd_hbm = bf16[1024,320]{1,0:T(8,128)(2,1)S(1)} copy(bf16[1024,320]{0,1:T(8,128)(2,1)} %param.19) | data formatting | bytes 1310720 | tf_op args[9]
  5.1 0.0 copy-done.2
  5.1 0.0 copy-done
  5.1 0.0 copy-done.1
  5.1 0.0 copy-done.7
  5.1 0.0 copy-start.3
  5.1 1.1 copy-done.3
  6.2 0.0 copy-start.4
  6.2 0.8 copy-done.4
  7.0 0.0 copy-start.5
  7.0 0.9 copy-done.5
  7.9 0.0 copy-start.6
  7.9 0.9 copy-done.6
  8.8 109.9 %shard_map.129 = (bf16[12,320]{1,0:T(8,128)(2,1)S(1)}, bf16[12,320]{1,0:T(8,128)(2,1)S(1)}, bf16[1,320,1024]{2,1,0:T(8,128)(2,1)S(1)}, bf16[1,320,1024]{2,1,0:T(8,128)(2,1)S(1)}) custom-call(bf16[96,320]{1,0:T(8,128)(2,1)S(1)} %copy-done.5, bf16[96,320]{1,0:T(8,128)(2,1)S(1)} %copy-done.6, s32[96,1]{1,0:T(8,128)S(1)} %copy-done.4, f32[96]{0:T(128)S(1)} %copy-done.7, ...), custom_call_target="tpu_custom_call" | custom-call | tf_op jit(solution)/shard_map/pallas_call | solution.py:325
  118.7 0.6 copy.21
  119.3 0.6 copy.22
  119.9 0.8 copy.23
  120.7 0.8 copy.24
Async XLA Ops:
  2.0 3.1 %copy-start.2 = (bf16[320,1024]{1,0:T(8,128)(2,1)S(1)}, bf16[320,1024]{1,0:T(8,128)(2,1)}, u32[]{:S(2)}) copy-start(bf16[320,1024]{1,0:T(8,128)(2,1)} %sg_hbm.1) | copy-start | bytes 1966084
  3.5 1.6 %copy-start = (bf16[1,320,1024]{2,1,0:T(8,128)(2,1)S(1)}, bf16[1,320,1024]{2,1,0:T(8,128)(2,1)}, u32[]{:S(2)}) copy-start(bf16[1,320,1024]{2,1,0:T(8,128)(2,1)} %eg_hbm.1) | copy-start | bytes 1966084
  3.5 1.6 %copy-start.1 = (bf16[1,320,1024]{2,1,0:T(8,128)(2,1)S(1)}, bf16[1,320,1024]{2,1,0:T(8,128)(2,1)}, u32[]{:S(2)}) copy-start(bf16[1,320,1024]{2,1,0:T(8,128)(2,1)} %eu_hbm.1) | copy-start | bytes 1966084
  3.5 1.6 %copy-start.7 = (f32[96]{0:T(128)S(1)}, f32[96]{0:T(128)}, u32[]{:S(2)}) copy-start(f32[96]{0:T(128)} %gate_hbm.1) | copy-start | bytes 1156
  5.1 1.1 copy-start.3
  6.2 0.8 copy-start.4
  7.0 0.9 copy-start.5
  7.9 0.9 copy-start.6

commit v2 on v1

v2 whole, which is shorter than its diff:
```python
import functools

import jax
import jax.numpy as jnp
from jax import lax
from jax.experimental import pallas as pl
from jax.experimental.pallas import tpu as pltpu
from jax.sharding import PartitionSpec as P

MESH = pl.DeviceIdType.MESH
F32 = jnp.float32
BF16 = jnp.bfloat16

TOK = 96
CAP = 24
NE = 8
NF = 16
ND = 8
SLOTS = NE * CAP
WIDTH = 320
HID = 1024
SUB = 48
COL = 128
STREAMS = 3
SUMS = ((0, 8, 4), (1, 7, 3), (0, 3, 1), (1, 2, 1))
SUM_AT = (0.0, 0.01, 2.5, 3.5)
SUM_TIME = 6.5
GATHERS = ((0, 1, 8), (1, 1, 7))
GATHER_AT = (0.0, 0.01)
GATHER_TIME = 8
LINKS = 8
JUMPS = sorted({1} | {near for _, _, near in SUMS} | {near for _, near, _ in GATHERS})
LEAD = 3
STAGGER = 0
SOURCES = ((0, 2, 4, 6), (1, 3, 5, 7))
LATE = 2
ROWS_DP = TOK // ND


def dot(a, b):
    return lax.dot_general(a, b, (((1,), (0,)), ((), ())), preferred_element_type=F32)


def dot_last(a, b):
    return lax.dot_general(a, b, (((1,), (1,)), ((), ())), preferred_element_type=F32)


def dot_first(a, b):
    return lax.dot_general(a, b, (((0,), (0,)), ((), ())), preferred_element_type=F32)


def kernel(
    tok_hbm, cot_hbm, routing_hbm, gate_hbm, eg_hbm, eu_hbm, ed_hbm, sg_hbm, su_hbm, sd_hbm,
    lo_hbm, gt_hbm, gg_hbm, gu_hbm,
    tok, cot, routing, gate, eg, eu, ed, sg, su, sd,
    outbox, inbox, routed_in, routed_cot, part_s, part_r,
    stage, held, act_s, act_r,
    outbox2, inbox2, term, outbox3, inbox3, lo, gt, gg, gu,
    load_sem, store_sem, rs_send, rs_recv, ag_send, ag_recv, x_send, x_recv, y_send, y_recv, z_send, z_recv,
):
    me_e, me_f, me_d = lax.axis_index("expert"), lax.axis_index("ffn"), lax.axis_index("dp")
    y_hi, core = lax.div(me_e, 2), lax.rem(me_e, 2)
    y_lo = lax.rem(me_d, 2)
    other_d = me_d + 1 - 2 * y_lo
    toward = 2 * y_lo - 1

    def way_of(way, stream):
        return 1 - way if stream == STREAMS - 1 else way

    def along(way, distance):
        return lax.rem(me_f + (distance if way == 0 else NF - distance), NF)

    def expert_at(dy, swap):
        return 2 * lax.rem(y_hi + dy + 4, 4) + (core if swap == 0 else 1 - core)

    loads = [
        pltpu.make_async_copy(src, dst, load_sem.at[n])
        for n, (src, dst) in enumerate(
            [
                (routing_hbm, routing), (gate_hbm, gate), (tok_hbm, tok), (cot_hbm, cot),
                (sg_hbm, sg), (su_hbm, su), (sd_hbm, sd),
                (eg_hbm.at[0], eg), (eu_hbm.at[0], eu), (ed_hbm.at[0], ed),
            ]
        )
    ]
    for load in loads:
        load.start()

    barrier = pltpu.get_barrier_semaphore()
    for jump in JUMPS:
        for way in range(2):
            pl.semaphore_signal(
                barrier, inc=1, device_id={"ffn": along(way, jump)}, device_id_type=MESH
            )
    for dy in (toward, 2):
        for swap in range(2):
            pl.semaphore_signal(
                barrier, inc=1, device_id={"expert": expert_at(dy, swap), "dp": other_d}, device_id_type=MESH
            )
    for k in range(1, NE):
        pl.semaphore_signal(
            barrier, inc=1, device_id={"expert": lax.rem(me_e + k, NE)}, device_id_type=MESH
        )
    for k in range(1, ND):
        pl.semaphore_signal(
            barrier, inc=1, device_id={"dp": lax.rem(me_d + k, ND)}, device_id_type=MESH
        )

    for n in range(4):
        loads[n].wait()

    same = (
        lax.broadcasted_iota(jnp.int32, (TOK, TOK), 0) == lax.broadcasted_iota(jnp.int32, (TOK, TOK), 1)
    )

    def column(row):
        across = jnp.broadcast_to(row.astype(F32).reshape(1, TOK), (TOK, TOK))
        return jnp.sum(jnp.where(same, across, 0.0), axis=1, keepdims=True)

    gate_column = column(gate[...])
    chosen = column(routing[...]).astype(jnp.int32)
    onehot = (chosen == lax.broadcasted_iota(jnp.int32, (TOK, NE), 1)).astype(F32)
    before = (
        lax.broadcasted_iota(jnp.int32, (TOK, TOK), 0) > lax.broadcasted_iota(jnp.int32, (TOK, TOK), 1)
    )
    earlier = dot(before.astype(BF16), onehot.astype(BF16))
    slot = jnp.sum(earlier * onehot, axis=1, keepdims=True).astype(jnp.int32)
    target = chosen * (2 * CAP) + slot
    boxes = lax.broadcasted_iota(jnp.int32, (TOK, 2 * SLOTS), 1)
    pick_first = (boxes == target).astype(BF16)
    pick_second = (boxes == target + CAP).astype(BF16)
    scaled = (gate_column * cot[...].astype(F32)).astype(BF16)
    outbox[...] = (dot_first(pick_first, tok[...]) + dot_first(pick_second, scaled)).astype(BF16)

    for n in range(4, 7):
        loads[n].wait()
    part_s[0] = dot(tok[...], sg[...])
    part_s[1] = dot(tok[...], su[...])
    part_s[2] = dot(cot[...], sd[...])

    pl.semaphore_wait(barrier, 2 * len(JUMPS) + 4 + (NE - 1) + (ND - 1))

    def box(ref, index):
        return ref.at[pl.ds(pl.multiple_of(index * 2 * CAP, 2 * CAP), 2 * CAP)]

    routes = [(0, 0, 1)] + [
        (dy, flip, swap) for dy, flip in ((toward, 1), (toward, 0), (2, 1)) for swap in range(2)
    ]

    def tokens_out(n):
        dy, flip, swap = routes[n]
        peer = expert_at(dy, swap)
        return pltpu.make_async_remote_copy(
            src_ref=box(outbox, peer), dst_ref=box(inbox, me_e),
            send_sem=x_send.at[n], recv_sem=x_recv.at[n],
            device_id={"expert": peer, "dp": other_d if flip else me_d}, device_id_type=MESH,
        )

    def tokens_in(n):
        dy, flip, swap = routes[n]
        peer = expert_at(dy if flip else -dy, swap)
        return pltpu.make_async_remote_copy(
            src_ref=box(outbox, me_e), dst_ref=box(inbox, peer),
            send_sem=x_send.at[n], recv_sem=x_recv.at[n],
            device_id={"expert": peer, "dp": other_d if flip else me_d}, device_id_type=MESH,
        )

    for n in range(len(routes)):
        tokens_out(n).start()
    box(inbox, me_e)[...] = box(outbox, me_e)[...]

    def block(ref, stream, owner):
        columns = pl.ds(pl.multiple_of(lax.div(owner, 2) * COL, COL), COL)
        half = lax.rem(owner, 2)
        first = half * SUB + (0 if stream == 0 else (stream - 1) * 2 * SUB)
        return ref.at[:, pl.ds(pl.multiple_of(first, SUB), SUB), columns]

    def mine(stream):
        return (part_s if stream == 0 else part_r), (act_s if stream == 0 else act_r)

    def sum_copy(stream, chain, step):
        way, far, near = SUMS[chain]
        way = way_of(way, stream)
        return pltpu.make_async_remote_copy(
            src_ref=stage.at[stream, chain, step], dst_ref=held.at[stream, chain, step],
            send_sem=rs_send.at[stream, chain, step], recv_sem=rs_recv.at[stream, chain, step],
            device_id={"ffn": along(way, 1 if step < far - near else near)}, device_id_type=MESH,
        )

    def sum_step(stream, chain, step):
        way, far, _ = SUMS[chain]
        way = way_of(way, stream)
        value = block(mine(stream)[0], stream, along(way, far - step))[...]
        if step > 0:
            sum_copy(stream, chain, step - 1).wait_recv()
            value = value + held[stream, chain, step - 1].astype(F32)
        stage[stream, chain, step] = value.astype(BF16)
        sum_copy(stream, chain, step).start()

    def sum_end(stream):
        part, act = mine(stream)
        value = block(part, stream, me_f)[...]
        for chain, (_, far, near) in sorted(enumerate(SUMS), reverse=True):
            sum_copy(stream, chain, far - near).wait_recv()
            value = value + held[stream, chain, far - near].astype(F32)
        g, u, p = value[0], value[1], value[2]
        squash = jax.nn.sigmoid(g)
        silu = g * squash
        own = block(act, stream, me_f)
        own[0] = (silu * u).astype(BF16)
        own[1] = (p * u * squash * (1.0 + g * (1.0 - squash))).astype(BF16)
        own[2] = (p * silu).astype(BF16)

    def gather_copy(stream, chain, step, distance):
        way, near, _ = GATHERS[chain]
        way = way_of(way, stream)
        ref = block(mine(stream)[1], stream, along(1 - way, distance))
        return pltpu.make_async_remote_copy(
            src_ref=ref, dst_ref=ref,
            send_sem=ag_send.at[stream, chain, step], recv_sem=ag_recv.at[stream, chain, step],
            device_id={"ffn": along(way, near if step == 0 else 1)}, device_id_type=MESH,
        )

    def gather_out(stream, chain, step):
        return gather_copy(stream, chain, step, 0 if step == 0 else GATHERS[chain][1] + step - 1)

    def gather_arrived(stream, chain, step):
        gather_copy(stream, chain, step, GATHERS[chain][1] + step).wait_recv()

    def gather_step(stream, chain, step):
        if step > 0:
            gather_arrived(stream, chain, step - 1)
        gather_out(stream, chain, step).start()

    def gather_end(stream):
        for chain, (_, near, far) in sorted(enumerate(GATHERS), reverse=True):
            gather_arrived(stream, chain, far - near)

    def routed_terms():
        for n in range(len(routes)):
            tokens_in(n).wait_recv()
        came = inbox[...].astype(F32)
        routed_in[...] = jnp.concatenate(
            [came[2 * CAP * e : 2 * CAP * e + CAP] for e in SOURCES[0] + SOURCES[1]], axis=0
        ).astype(BF16)
        routed_cot[...] = jnp.concatenate(
            [came[2 * CAP * e + CAP : 2 * CAP * (e + 1)] for e in SOURCES[0] + SOURCES[1]], axis=0
        ).astype(BF16)
        for n in range(7, 10):
            loads[n].wait()
        part_r[0] = dot(routed_in[...], eg[...])
        part_r[1] = dot(routed_in[...], eu[...])
        part_r[2] = dot(routed_cot[...], ed[...])

    def result_copy(peer, sender):
        return pltpu.make_async_remote_copy(
            src_ref=box(outbox2, peer), dst_ref=box(inbox2, sender),
            send_sem=y_send.at[peer], recv_sem=y_recv.at[sender],
            device_id={"expert": peer}, device_id_type=MESH,
        )

    def routed_results(part):
        rows = slice(part * 2 * SUB, (part + 1) * 2 * SUB)
        routed_out = dot_last(act_r[0, rows], ed[...])
        routed_back = dot_last(act_r[1, rows], eg[...]) + dot_last(act_r[2, rows], eu[...])
        for n, e in enumerate(SOURCES[part]):
            outbox2[2 * CAP * e : 2 * CAP * (e + 1)] = jnp.concatenate(
                [routed_out[CAP * n : CAP * (n + 1)], routed_back[CAP * n : CAP * (n + 1)]], axis=0
            ).astype(BF16)

            @pl.when(me_e != e)
            def _():
                result_copy(e, me_e).start()

            @pl.when(me_e == e)
            def _():
                box(inbox2, e)[...] = box(outbox2, e)[...]

    begins = (0, LEAD + 0.1, LEAD + STAGGER + 0.2)
    routed_end = begins[2] + SUM_TIME + GATHER_TIME
    plan = [(LEAD - 0.5, "Rterms", routed_terms)]
    for stream, begin in enumerate(begins):
        second = begin + SUM_TIME if stream > 0 else routed_end - GATHER_TIME + LATE
        if stream > 0:
            plan.append((second + GATHER_TIME + 0.05, f"Rout{stream}", functools.partial(routed_results, stream - 1)))
        plan.append((begin + SUM_TIME - 0.05, f"Aend{stream}", functools.partial(sum_end, stream)))
        plan.append((second + GATHER_TIME, f"Gend{stream}", functools.partial(gather_end, stream)))
        for chain, (_, far, near) in enumerate(SUMS):
            for step in range(far - near + 1):
                when = begin + SUM_AT[chain] + step
                plan.append((when, f"A{stream}{chain}{step}", functools.partial(sum_step, stream, chain, step)))
        for chain, (_, near, far) in enumerate(GATHERS):
            for step in range(far - near + 1):
                when = second + GATHER_AT[chain] + step
                plan.append((when, f"G{stream}{chain}{step}", functools.partial(gather_step, stream, chain, step)))
    for _, name, act in sorted(plan, key=lambda entry: entry[0]):
        act()

    shared_out = dot_last(act_s[0], sd[...])
    shared_back = dot_last(act_s[1], sg[...]) + dot_last(act_s[2], su[...])
    for k in range(1, NE):
        result_copy(me_e, lax.rem(me_e + k, NE)).wait_recv()
    term[0] = gate_column * dot(pick_first, inbox2[...]) + shared_out
    term[1] = dot(pick_second, inbox2[...]) + shared_back
    for d in range(ND):
        outbox3[d, :ROWS_DP] = term[0, ROWS_DP * d : ROWS_DP * (d + 1)]
        outbox3[d, ROWS_DP:] = term[1, ROWS_DP * d : ROWS_DP * (d + 1)]

    def dp_send(k):
        peer = lax.rem(me_d + k, ND)
        return pltpu.make_async_remote_copy(
            src_ref=outbox3.at[peer], dst_ref=inbox3.at[k],
            send_sem=z_send.at[k], recv_sem=z_recv.at[k],
            device_id={"dp": peer}, device_id_type=MESH,
        )

    for k in range(1, ND):
        dp_send(k).start()

    gg[...] = dot_first(routed_in[...], act_r[1]).astype(BF16)
    gu[...] = dot_first(routed_in[...], act_r[2]).astype(BF16)
    stores = [
        pltpu.make_async_copy(gg, gg_hbm.at[0], store_sem.at[0]),
        pltpu.make_async_copy(gu, gu_hbm.at[0], store_sem.at[1]),
    ]
    for store in stores:
        store.start()

    total = outbox3[me_d]
    for k in range(1, ND):
        dp_send(k).wait_recv()
        total = total + inbox3[k]
    lo[...] = total[:ROWS_DP].astype(BF16)
    gt[...] = total[ROWS_DP:].astype(BF16)
    last = [
        pltpu.make_async_copy(lo, lo_hbm, store_sem.at[2]),
        pltpu.make_async_copy(gt, gt_hbm, store_sem.at[3]),
    ]
    for store in last:
        store.start()
    for stream in range(STREAMS):
        for chain, (_, far, near) in enumerate(SUMS):
            for step in range(far - near + 1):
                sum_copy(stream, chain, step).wait_send()
        for chain, (_, near, far) in enumerate(GATHERS):
            for step in range(far - near + 1):
                gather_out(stream, chain, step).wait_send()
    for n in range(len(routes)):
        tokens_out(n).wait_send()
    for k in range(1, NE):
        result_copy(lax.rem(me_e + k, NE), me_e).wait_send()
    for k in range(1, ND):
        dp_send(k).wait_send()
    for store in stores + last:
        store.wait()


def place(*refs):
    n = (len(refs) - 1) // 3
    sources, results, held, sem = refs[:n], refs[n : 2 * n], refs[2 * n : 3 * n], refs[-1]
    reads = [pltpu.make_async_copy(sources[k], held[k], sem.at[0, k]) for k in range(n)]
    writes = [pltpu.make_async_copy(held[k], results[k], sem.at[1, k]) for k in range(n)]
    for read in reads:
        read.start()
    for read, write in zip(reads, writes):
        read.wait()
        write.start()
    for write in writes:
        write.wait()


def per_device(tokens, cotangent, routing, gate_value, eg, eu, ed, sg, su, sd):
    args = (
        tokens, cotangent, routing.reshape(TOK), gate_value,
        eg, eu, jnp.swapaxes(ed, 1, 2), sg, su, jnp.swapaxes(sd, 0, 1),
    )
    vmem = pltpu.VMEM
    dma = pltpu.SemaphoreType.DMA
    any_spec = pl.BlockSpec(memory_space=pl.ANY)
    hbm_spec = pl.BlockSpec(memory_space=pltpu.HBM)
    results = pl.pallas_call(
        kernel,
        out_shape=(
            jax.ShapeDtypeStruct((ROWS_DP, WIDTH), BF16),
            jax.ShapeDtypeStruct((ROWS_DP, WIDTH), BF16),
            jax.ShapeDtypeStruct((1, WIDTH, HID), BF16),
            jax.ShapeDtypeStruct((1, WIDTH, HID), BF16),
        ),
        in_specs=[hbm_spec] * 10,
        out_specs=(any_spec,) * 4,
        scratch_shapes=[
            vmem((TOK, WIDTH), BF16), vmem((TOK, WIDTH), BF16), vmem((TOK,), jnp.int32), vmem((TOK,), F32),
            vmem((WIDTH, HID), BF16), vmem((WIDTH, HID), BF16), vmem((WIDTH, HID), BF16),
            vmem((WIDTH, HID), BF16), vmem((WIDTH, HID), BF16), vmem((WIDTH, HID), BF16),
            vmem((2 * SLOTS, WIDTH), BF16), vmem((2 * SLOTS, WIDTH), BF16),
            vmem((SLOTS, WIDTH), BF16), vmem((SLOTS, WIDTH), BF16),
            vmem((3, TOK, HID), F32), vmem((3, SLOTS, HID), F32),
            vmem((STREAMS, len(SUMS), LINKS, 3, SUB, COL), BF16),
            vmem((STREAMS, len(SUMS), LINKS, 3, SUB, COL), BF16),
            vmem((3, TOK, HID), BF16), vmem((3, SLOTS, HID), BF16),
            vmem((2 * SLOTS, WIDTH), BF16), vmem((2 * SLOTS, WIDTH), BF16),
            vmem((2, TOK, WIDTH), F32),
            vmem((ND, 2 * ROWS_DP, WIDTH), F32), vmem((ND, 2 * ROWS_DP, WIDTH), F32),
            vmem((ROWS_DP, WIDTH), BF16), vmem((ROWS_DP, WIDTH), BF16),
            vmem((WIDTH, HID), BF16), vmem((WIDTH, HID), BF16),
            dma((10,)), dma((4,)),
            dma((STREAMS, len(SUMS), LINKS)), dma((STREAMS, len(SUMS), LINKS)),
            dma((STREAMS, len(GATHERS), LINKS)), dma((STREAMS, len(GATHERS), LINKS)),
            dma((NE,)), dma((NE,)), dma((NE,)), dma((NE,)), dma((ND,)), dma((ND,)),
        ],
        compiler_params=pltpu.CompilerParams(
            collective_id=0, has_side_effects=True, vmem_limit_bytes=60 * 1024 * 1024
        ),
    )(*args)
    return pl.pallas_call(
        place,
        out_shape=tuple(jax.ShapeDtypeStruct(part.shape, part.dtype) for part in results),
        in_specs=[any_spec] * 4,
        out_specs=(hbm_spec,) * 4,
        scratch_shapes=[vmem(part.shape, part.dtype) for part in results] + [dma((2, 4))],
        compiler_params=pltpu.CompilerParams(vmem_limit_bytes=60 * 1024 * 1024),
    )(*results)


def solution(mesh):
    placed = (
        P("expert", "ffn"),
        P("expert", "ffn"),
        P("expert", None),
        P("expert"),
        P("expert", "ffn", "dp"),
        P("expert", "ffn", "dp"),
        P("expert", "dp", "ffn"),
        P("ffn", "dp"),
        P("ffn", "dp"),
        P("dp", "ffn"),
    )
    return jax.shard_map(
        per_device,
        mesh=mesh,
        in_specs=placed,
        out_specs=(
            P(("expert", "dp"), "ffn"),
            P(("expert", "dp"), "ffn"),
            P("expert", "ffn", "dp"),
            P("expert", "ffn", "dp"),
        ),
        check_vma=False,
    )
```

time: 122 us -> 104 us (0.85)
  the two profiles are of different devices: /device:TPU:14 before, /device:TPU:1 now
where the time goes in v2:
time: 104 us
  Pallas kernels  103 us (99%)
    pallas_call x1, Pallas kernels, per_device(): pl.pallas_call(kernel, out_shape=(jax.ShapeDtypeStruct((ROWS_DP, WIDTH),...  101 us
    pallas_call x1, Pallas kernels, per_device(): pl.pallas_call(place, out_shape=tuple((jax.ShapeDtypeStruct(part.shape, p...  2.24 us

profile of v2, /device:TPU:1, one launch (start us, length us, event | category | flops | bytes accessed | tf_op | source)
XLA Modules:
  0.0 103.7 jit_solution(16871740594437437420)
XLA Ops:
  0.6 100.8 %shard_map.129 = (bf16[12,320]{1,0:T(8,128)(2,1)}, bf16[12,320]{1,0:T(8,128)(2,1)}, bf16[1,320,1024]{2,1,0:T(8,128)(2,1)}, bf16[1,320,1024]{2,1,0:T(8,128)(2,1)}) custom-call(bf16[96,320]{1,0:T(8,128)(2,1)} %tok_hbm.1, bf16[96,320]{1,0:T(8,128)(2,1)} %cot_hbm.1, s32[96]{0:T(128)} %bitcast.5, f32[96]{0:T(128)} %gate_hbm.1, bf16[1,320,1024]{2,1,0:T(8,128)(2,1)} %eg_hbm.1, ...), custom_call_target="tpu_custom_call" | custom-call | tf_op jit(solution)/shard_map/pallas_call | solution.py:381
  101.4 2.2 %shard_map.130 = (bf16[12,320]{1,0:T(8,128)(2,1)}, bf16[12,320]{1,0:T(8,128)(2,1)}, bf16[1,320,1024]{2,1,0:T(8,128)(2,1)}, bf16[1,320,1024]{2,1,0:T(8,128)(2,1)}) custom-call(bf16[12,320]{1,0:T(8,128)(2,1)} %get-tuple-element.8.refs_0_, bf16[12,320]{1,0:T(8,128)(2,1)} %get-tuple-element.9.refs_1_, bf16[1,320,1024]{2,1,0:T(8,128)(2,1)} %get-tuple-element.10.refs_2_, ...), custom_call_target="tpu_custom_call" | custom-call | tf_op jit(solution)/shard_map/pallas_call | solution.py:415

commit v3 on v2

--- a/solution.py
+++ b/solution.py
@@ -1,4 +1,5 @@
 import functools
+from typing import NamedTuple
 
 import jax
 import jax.numpy as jnp
@@ -22,19 +23,37 @@
 SUB = 48
 COL = 128
 STREAMS = 3
-SUMS = ((0, 8, 4), (1, 7, 3), (0, 3, 1), (1, 2, 1))
-SUM_AT = (0.0, 0.01, 2.5, 3.5)
-SUM_TIME = 6.5
-GATHERS = ((0, 1, 8), (1, 1, 7))
-GATHER_AT = (0.0, 0.01)
-GATHER_TIME = 8
+SOURCES = ((0, 2, 4, 6), (1, 3, 5, 7))
 LINKS = 8
-JUMPS = sorted({1} | {near for _, _, near in SUMS} | {near for _, near, _ in GATHERS})
-LEAD = 3
-STAGGER = 0
-SOURCES = ((0, 2, 4, 6), (1, 3, 5, 7))
-LATE = 2
+CHAINS = 4
+
+
+class Ring(NamedTuple):
+    sums: tuple
+    sum_at: tuple
+    sum_time: float
+    gathers: tuple
+    gather_at: tuple
+    gather_time: float
+    lead: float
+    late: float
+
+
+RINGS = (
+    Ring(
+        ((0, 8, 4), (1, 7, 3), (0, 3, 1), (1, 2, 1)), (0.0, 0.01, 0.2, 1.2), 6.5,
+        ((0, 4, 8), (1, 4, 7), (0, 1, 3), (1, 1, 3)), (0.0, 0.01, 0.02, 0.03), 5.5,
+        3, 1,
+    ),
+    Ring(
+        ((0, 8, 4), (1, 7, 3), (0, 3, 1), (1, 2, 1)), (0.0, 0.01, 0.2, 1.2), 6.5,
+        ((0, 1, 8), (1, 1, 7)), (0.0, 0.01), 8,
+        3, 2,
+    ),
+)
+JUMPS = sorted({1} | {near for ring in RINGS for _, _, near in ring.sums} | {near for ring in RINGS for _, near, _ in ring.gathers})
 ROWS_DP = TOK // ND
+PARTNERS = ((0, 0, 1),) + tuple((dy, flip, swap) for dy, flip in ((1, 0), (1, 1), (-1, 0), (2, 1)) for swap in (0, 1))
 
 
 def dot(a, b):
@@ -73,6 +92,22 @@
     def expert_at(dy, swap):
         return 2 * lax.rem(y_hi + dy + 4, 4) + (core if swap == 0 else 1 - core)
 
+    barrier = pltpu.get_barrier_semaphore()
+    for jump in JUMPS:
+        for way in range(2):
+            pl.semaphore_signal(
+                barrier, inc=1, device_id={"ffn": along(way, jump)}, device_id_type=MESH
+            )
+    for dy, flip, swap in PARTNERS:
+        pl.semaphore_signal(
+            barrier, inc=1,
+            device_id={"expert": expert_at(dy * toward, swap), "dp": other_d if flip else me_d}, device_id_type=MESH,
+        )
+    for k in range(1, ND):
+        pl.semaphore_signal(
+            barrier, inc=1, device_id={"dp": lax.rem(me_d + k, ND)}, device_id_type=MESH
+        )
+
     loads = [
         pltpu.make_async_copy(src, dst, load_sem.at[n])
         for n, (src, dst) in enumerate(
@@ -86,26 +121,6 @@
     for load in loads:
         load.start()
 
-    barrier = pltpu.get_barrier_semaphore()
-    for jump in JUMPS:
-        for way in range(2):
-            pl.semaphore_signal(
-                barrier, inc=1, device_id={"ffn": along(way, jump)}, device_id_type=MESH
-            )
-    for dy in (toward, 2):
-        for swap in range(2):
-            pl.semaphore_signal(
-                barrier, inc=1, device_id={"expert": expert_at(dy, swap), "dp": other_d}, device_id_type=MESH
-            )
-    for k in range(1, NE):
-        pl.semaphore_signal(
-            barrier, inc=1, device_id={"expert": lax.rem(me_e + k, NE)}, device_id_type=MESH
-        )
-    for k in range(1, ND):
-        pl.semaphore_signal(
-            barrier, inc=1, device_id={"dp": lax.rem(me_d + k, ND)}, device_id_type=MESH
-        )
-
     for n in range(4):
         loads[n].wait()
 
@@ -118,27 +133,21 @@
         return jnp.sum(jnp.where(same, across, 0.0), axis=1, keepdims=True)
 
     gate_column = column(gate[...])
-    chosen = column(routing[...]).astype(jnp.int32)
-    onehot = (chosen == lax.broadcasted_iota(jnp.int32, (TOK, NE), 1)).astype(F32)
+    chosen = routing[...].reshape(1, TOK)
+    onehot = (chosen == lax.broadcasted_iota(jnp.int32, (NE, TOK), 0)).astype(F32)
     before = (
-        lax.broadcasted_iota(jnp.int32, (TOK, TOK), 0) > lax.broadcasted_iota(jnp.int32, (TOK, TOK), 1)
+        lax.broadcasted_iota(jnp.int32, (TOK, TOK), 0) < lax.broadcasted_iota(jnp.int32, (TOK, TOK), 1)
     )
-    earlier = dot(before.astype(BF16), onehot.astype(BF16))
-    slot = jnp.sum(earlier * onehot, axis=1, keepdims=True).astype(jnp.int32)
-    target = chosen * (2 * CAP) + slot
-    boxes = lax.broadcasted_iota(jnp.int32, (TOK, 2 * SLOTS), 1)
+    earlier = dot(onehot.astype(BF16), before.astype(BF16))
+    slot = jnp.sum(earlier * onehot, axis=0, keepdims=True)
+    target = chosen * (2 * CAP) + slot.astype(jnp.int32)
+    boxes = lax.broadcasted_iota(jnp.int32, (2 * SLOTS, TOK), 0)
     pick_first = (boxes == target).astype(BF16)
     pick_second = (boxes == target + CAP).astype(BF16)
     scaled = (gate_column * cot[...].astype(F32)).astype(BF16)
-    outbox[...] = (dot_first(pick_first, tok[...]) + dot_first(pick_second, scaled)).astype(BF16)
-
-    for n in range(4, 7):
-        loads[n].wait()
-    part_s[0] = dot(tok[...], sg[...])
-    part_s[1] = dot(tok[...], su[...])
-    part_s[2] = dot(cot[...], sd[...])
-
-    pl.semaphore_wait(barrier, 2 * len(JUMPS) + 4 + (NE - 1) + (ND - 1))
+    outbox[...] = (dot(pick_first, tok[...]) + dot(pick_second, scaled)).astype(BF16)
+
+    pl.semaphore_wait(barrier, 2 * len(JUMPS) + len(PARTNERS) + (ND - 1))
 
     def box(ref, index):
         return ref.at[pl.ds(pl.multiple_of(index * 2 * CAP, 2 * CAP), 2 * CAP)]
@@ -169,6 +178,12 @@
         tokens_out(n).start()
     box(inbox, me_e)[...] = box(outbox, me_e)[...]
 
+    for n in range(4, 7):
+        loads[n].wait()
+    part_s[0] = dot(tok[...], sg[...])
+    part_s[1] = dot(tok[...], su[...])
+    part_s[2] = dot(cot[...], sd[...])
+
     def block(ref, stream, owner):
         columns = pl.ds(pl.multiple_of(lax.div(owner, 2) * COL, COL), COL)
         half = lax.rem(owner, 2)
@@ -178,8 +193,8 @@
     def mine(stream):
         return (part_s if stream == 0 else part_r), (act_s if stream == 0 else act_r)
 
-    def sum_copy(stream, chain, step):
-        way, far, near = SUMS[chain]
+    def sum_copy(ring, stream, chain, step):
+        way, far, near = ring.sums[chain]
         way = way_of(way, stream)
         return pltpu.make_async_remote_copy(
             src_ref=stage.at[stream, chain, step], dst_ref=held.at[stream, chain, step],
@@ -187,21 +202,21 @@
             device_id={"ffn": along(way, 1 if step < far - near else near)}, device_id_type=MESH,
         )
 
-    def sum_step(stream, chain, step):
-        way, far, _ = SUMS[chain]
+    def sum_step(ring, stream, chain, step):
+        way, far, _ = ring.sums[chain]
         way = way_of(way, stream)
         value = block(mine(stream)[0], stream, along(way, far - step))[...]
         if step > 0:
-            sum_copy(stream, chain, step - 1).wait_recv()
+            sum_copy(ring, stream, chain, step - 1).wait_recv()
             value = value + held[stream, chain, step - 1].astype(F32)
         stage[stream, chain, step] = value.astype(BF16)
-        sum_copy(stream, chain, step).start()
-
-    def sum_end(stream):
+        sum_copy(ring, stream, chain, step).start()
+
+    def sum_end(ring, stream):
         part, act = mine(stream)
         value = block(part, stream, me_f)[...]
-        for chain, (_, far, near) in sorted(enumerate(SUMS), reverse=True):
-            sum_copy(stream, chain, far - near).wait_recv()
+        for chain, (_, far, near) in sorted(enumerate(ring.sums), reverse=True):
+            sum_copy(ring, stream, chain, far - near).wait_recv()
             value = value + held[stream, chain, far - near].astype(F32)
         g, u, p = value[0], value[1], value[2]
         squash = jax.nn.sigmoid(g)
@@ -211,8 +226,8 @@
         own[1] = (p * u * squash * (1.0 + g * (1.0 - squash))).astype(BF16)
         own[2] = (p * silu).astype(BF16)
 
-    def gather_copy(stream, chain, step, distance):
-        way, near, _ = GATHERS[chain]
+    def gather_copy(ring, stream, chain, step, distance):
+        way, near, _ = ring.gathers[chain]
         way = way_of(way, stream)
         ref = block(mine(stream)[1], stream, along(1 - way, distance))
         return pltpu.make_async_remote_copy(
@@ -221,20 +236,20 @@
             device_id={"ffn": along(way, near if step == 0 else 1)}, device_id_type=MESH,
         )
 
-    def gather_out(stream, chain, step):
-        return gather_copy(stream, chain, step, 0 if step == 0 else GATHERS[chain][1] + step - 1)
-
-    def gather_arrived(stream, chain, step):
-        gather_copy(stream, chain, step, GATHERS[chain][1] + step).wait_recv()
-
-    def gather_step(stream, chain, step):
+    def gather_out(ring, stream, chain, step):
+        return gather_copy(ring, stream, chain, step, 0 if step == 0 else ring.gathers[chain][1] + step - 1)
+
+    def gather_arrived(ring, stream, chain, step):
+        gather_copy(ring, stream, chain, step, ring.gathers[chain][1] + step).wait_recv()
+
+    def gather_step(ring, stream, chain, step):
         if step > 0:
-            gather_arrived(stream, chain, step - 1)
-        gather_out(stream, chain, step).start()
-
-    def gather_end(stream):
-        for chain, (_, near, far) in sorted(enumerate(GATHERS), reverse=True):
-            gather_arrived(stream, chain, far - near)
+            gather_arrived(ring, stream, chain, step - 1)
+        gather_out(ring, stream, chain, step).start()
+
+    def gather_end(ring, stream):
+        for chain, (_, near, far) in sorted(enumerate(ring.gathers), reverse=True):
+            gather_arrived(ring, stream, chain, far - near)
 
     def routed_terms():
         for n in range(len(routes)):
@@ -252,12 +267,23 @@
         part_r[1] = dot(routed_in[...], eu[...])
         part_r[2] = dot(routed_cot[...], ed[...])
 
-    def result_copy(peer, sender):
+    def result_copy(part, dy):
+        peer = 2 * lax.rem(y_hi + dy, 4) + part
+        swap = lax.rem(core + part, 2)
+        place = (1, 2 + 2 * y_lo + swap, 6 + swap, 2 + 2 * y_lo + swap)[dy]
+        where = (me_d, me_d - y_lo, other_d, me_d - y_lo + 1)[dy]
         return pltpu.make_async_remote_copy(
-            src_ref=box(outbox2, peer), dst_ref=box(inbox2, sender),
-            send_sem=y_send.at[peer], recv_sem=y_recv.at[sender],
-            device_id={"expert": peer}, device_id_type=MESH,
-        )
+            src_ref=box(outbox2, peer), dst_ref=box(inbox2, place),
+            send_sem=y_send.at[2 * dy + part], recv_sem=y_recv.at[place],
+            device_id={"expert": peer, "dp": where}, device_id_type=MESH,
+        )
+
+    def result_arrived(n):
+        pltpu.make_async_remote_copy(
+            src_ref=box(outbox2, n), dst_ref=box(inbox2, n),
+            send_sem=y_send.at[n], recv_sem=y_recv.at[n],
+            device_id={"expert": expert_at(0, 1)}, device_id_type=MESH,
+        ).wait_recv()
 
     def routed_results(part):
         rows = slice(part * 2 * SUB, (part + 1) * 2 * SUB)
@@ -268,40 +294,59 @@
                 [routed_out[CAP * n : CAP * (n + 1)], routed_back[CAP * n : CAP * (n + 1)]], axis=0
             ).astype(BF16)
 
-            @pl.when(me_e != e)
-            def _():
-                result_copy(e, me_e).start()
-
-            @pl.when(me_e == e)
-            def _():
-                box(inbox2, e)[...] = box(outbox2, e)[...]
-
-    begins = (0, LEAD + 0.1, LEAD + STAGGER + 0.2)
-    routed_end = begins[2] + SUM_TIME + GATHER_TIME
-    plan = [(LEAD - 0.5, "Rterms", routed_terms)]
-    for stream, begin in enumerate(begins):
-        second = begin + SUM_TIME if stream > 0 else routed_end - GATHER_TIME + LATE
-        if stream > 0:
-            plan.append((second + GATHER_TIME + 0.05, f"Rout{stream}", functools.partial(routed_results, stream - 1)))
-        plan.append((begin + SUM_TIME - 0.05, f"Aend{stream}", functools.partial(sum_end, stream)))
-        plan.append((second + GATHER_TIME, f"Gend{stream}", functools.partial(gather_end, stream)))
-        for chain, (_, far, near) in enumerate(SUMS):
-            for step in range(far - near + 1):
-                when = begin + SUM_AT[chain] + step
-                plan.append((when, f"A{stream}{chain}{step}", functools.partial(sum_step, stream, chain, step)))
-        for chain, (_, near, far) in enumerate(GATHERS):
-            for step in range(far - near + 1):
-                when = second + GATHER_AT[chain] + step
-                plan.append((when, f"G{stream}{chain}{step}", functools.partial(gather_step, stream, chain, step)))
-    for _, name, act in sorted(plan, key=lambda entry: entry[0]):
-        act()
+        for dy in range(1, 4):
+            result_copy(part, dy).start()
+
+        @pl.when(core != part)
+        def _():
+            result_copy(part, 0).start()
+
+        @pl.when(core == part)
+        def _():
+            inbox2[: 2 * CAP] = box(outbox2, me_e)[...]
+
+    def run(ring):
+        begins = (0, ring.lead + 0.1, ring.lead + 0.2)
+        routed_end = ring.lead + ring.sum_time + ring.gather_time + 0.2
+        plan = [(ring.lead - 0.5, "Rterms", routed_terms)]
+        for stream, begin in enumerate(begins):
+            second = begin + ring.sum_time if stream > 0 else routed_end - ring.gather_time + ring.late
+            if stream > 0:
+                results = functools.partial(routed_results, stream - 1)
+                plan.append((second + ring.gather_time + 0.05, f"Rout{stream}", results))
+            plan.append((begin + ring.sum_time - 0.05, f"Aend{stream}", functools.partial(sum_end, ring, stream)))
+            plan.append((second + ring.gather_time, f"Gend{stream}", functools.partial(gather_end, ring, stream)))
+            for chain, (_, far, near) in enumerate(ring.sums):
+                for step in range(far - near + 1):
+                    when = begin + ring.sum_at[chain] + step
+                    plan.append((when, f"A{stream}{chain}{step}", functools.partial(sum_step, ring, stream, chain, step)))
+            for chain, (_, near, far) in enumerate(ring.gathers):
+                for step in range(far - near + 1):
+                    when = second + ring.gather_at[chain] + step
+                    plan.append((when, f"G{stream}{chain}{step}", functools.partial(gather_step, ring, stream, chain, step)))
+        for _, name, act in sorted(plan, key=lambda entry: entry[0]):
+            act()
+
+    for side in range(2):
+        pl.when(core == side)(functools.partial(run, RINGS[side]))
 
     shared_out = dot_last(act_s[0], sd[...])
     shared_back = dot_last(act_s[1], sg[...]) + dot_last(act_s[2], su[...])
-    for k in range(1, NE):
-        result_copy(me_e, lax.rem(me_e + k, NE)).wait_recv()
-    term[0] = gate_column * dot(pick_first, inbox2[...]) + shared_out
-    term[1] = dot(pick_second, inbox2[...]) + shared_back
+    senders = [me_e, expert_at(0, 1)] + [expert_at(toward, n % 2) for n in range(4)] + [expert_at(2, n) for n in range(2)]
+    columns = lax.broadcasted_iota(jnp.int32, (1, 2 * SLOTS), 1)
+    sender = jnp.zeros((1, 2 * SLOTS), jnp.int32)
+    for n in range(NE):
+        here = (columns >= 2 * CAP * n) & (columns < 2 * CAP * (n + 1))
+        sender = jnp.where(here, senders[n], sender)
+    row = lax.rem(columns, 2 * CAP)
+    slot_column = column(slot).astype(jnp.int32)
+    of_sender = column(chosen).astype(jnp.int32) == sender
+    take_first = (of_sender & (row == slot_column)).astype(BF16)
+    take_second = (of_sender & (row == slot_column + CAP)).astype(BF16)
+    for n in range(1, NE):
+        result_arrived(n)
+    term[0] = gate_column * dot(take_first, inbox2[...]) + shared_out
+    term[1] = dot(take_second, inbox2[...]) + shared_back
     for d in range(ND):
         outbox3[d, :ROWS_DP] = term[0, ROWS_DP * d : ROWS_DP * (d + 1)]
         outbox3[d, ROWS_DP:] = term[1, ROWS_DP * d : ROWS_DP * (d + 1)]
@@ -338,17 +383,27 @@
     ]
     for store in last:
         store.start()
-    for stream in range(STREAMS):
-        for chain, (_, far, near) in enumerate(SUMS):
-            for step in range(far - near + 1):
-                sum_copy(stream, chain, step).wait_send()
-        for chain, (_, near, far) in enumerate(GATHERS):
-            for step in range(far - near + 1):
-                gather_out(stream, chain, step).wait_send()
+    def all_sent(ring):
+        for stream in range(STREAMS):
+            for chain, (_, far, near) in enumerate(ring.sums):
+                for step in range(far - near + 1):
+                    sum_copy(ring, stream, chain, step).wait_send()
+            for chain, (_, near, far) in enumerate(ring.gathers):
+                for step in range(far - near + 1):
+                    gather_out(ring, stream, chain, step).wait_send()
+
+    for side in range(2):
+        pl.when(core == side)(functools.partial(all_sent, RINGS[side]))
     for n in range(len(routes)):
         tokens_out(n).wait_send()
-    for k in range(1, NE):
-        result_copy(lax.rem(me_e + k, NE), me_e).wait_send()
+    for part in range(2):
+        for dy in range(1, 4):
+            result_copy(part, dy).wait_send()
+
+        @pl.when(core != part)
+        def _(part=part):
+            result_copy(part, 0).wait_send()
+
     for k in range(1, ND):
         dp_send(k).wait_send()
     for store in stores + last:
@@ -395,8 +450,8 @@
             vmem((2 * SLOTS, WIDTH), BF16), vmem((2 * SLOTS, WIDTH), BF16),
             vmem((SLOTS, WIDTH), BF16), vmem((SLOTS, WIDTH), BF16),
             vmem((3, TOK, HID), F32), vmem((3, SLOTS, HID), F32),
-            vmem((STREAMS, len(SUMS), LINKS, 3, SUB, COL), BF16),
-            vmem((STREAMS, len(SUMS), LINKS, 3, SUB, COL), BF16),
+            vmem((STREAMS, CHAINS, LINKS, 3, SUB, COL), BF16),
+            vmem((STREAMS, CHAINS, LINKS, 3, SUB, COL), BF16),
             vmem((3, TOK, HID), BF16), vmem((3, SLOTS, HID), BF16),
             vmem((2 * SLOTS, WIDTH), BF16), vmem((2 * SLOTS, WIDTH), BF16),
             vmem((2, TOK, WIDTH), F32),
@@ -404,8 +459,8 @@
             vmem((ROWS_DP, WIDTH), BF16), vmem((ROWS_DP, WIDTH), BF16),
             vmem((WIDTH, HID), BF16), vmem((WIDTH, HID), BF16),
             dma((10,)), dma((4,)),
-            dma((STREAMS, len(SUMS), LINKS)), dma((STREAMS, len(SUMS), LINKS)),
-            dma((STREAMS, len(GATHERS), LINKS)), dma((STREAMS, len(GATHERS), LINKS)),
+            dma((STREAMS, CHAINS, LINKS)), dma((STREAMS, CHAINS, LINKS)),
+            dma((STREAMS, CHAINS, LINKS)), dma((STREAMS, CHAINS, LINKS)),
             dma((NE,)), dma((NE,)), dma((NE,)), dma((NE,)), dma((ND,)), dma((ND,)),
         ],
         compiler_params=pltpu.CompilerParams(

time: 104 us -> 103 us (level)
    pallas_call x1, Pallas kernels: 101 us -> 99.5 us  [per_device(): pl.pallas_call(kernel, out_shape=(jax.ShapeDtypeStruct((ROWS_DP, WIDTH),...]
where the time goes in v3:
time: 103 us; the launch traced here: 102 us
  Pallas kernels  102 us (99%)
    pallas_call x1, Pallas kernels, per_device(): pl.pallas_call(kernel, out_shape=(jax.ShapeDtypeStruct((ROWS_DP, WIDTH),...  99.5 us
    pallas_call x1, Pallas kernels, per_device(): pl.pallas_call(place, out_shape=tuple((jax.ShapeDtypeStruct(part.shape, p...  2.24 us

profile of v3, /device:TPU:1, one launch (start us, length us, event | category | flops | bytes accessed | tf_op | source)
XLA Modules:
  0.0 102.4 jit_solution(12935596073008110970)
XLA Ops:
  0.6 99.5 %shard_map.129 = (bf16[12,320]{1,0:T(8,128)(2,1)}, bf16[12,320]{1,0:T(8,128)(2,1)}, bf16[1,320,1024]{2,1,0:T(8,128)(2,1)}, bf16[1,320,1024]{2,1,0:T(8,128)(2,1)}) custom-call(bf16[96,320]{1,0:T(8,128)(2,1)} %tok_hbm.1, bf16[96,320]{1,0:T(8,128)(2,1)} %cot_hbm.1, s32[96]{0:T(128)} %bitcast.5, f32[96]{0:T(128)} %gate_hbm.1, bf16[1,320,1024]{2,1,0:T(8,128)(2,1)} %eg_hbm.1, ...), custom_call_target="tpu_custom_call" | custom-call | tf_op jit(solution)/shard_map/pallas_call | solution.py:436
  100.1 2.2 %shard_map.130 = (bf16[12,320]{1,0:T(8,128)(2,1)}, bf16[12,320]{1,0:T(8,128)(2,1)}, bf16[1,320,1024]{2,1,0:T(8,128)(2,1)}, bf16[1,320,1024]{2,1,0:T(8,128)(2,1)}) custom-call(bf16[12,320]{1,0:T(8,128)(2,1)} %get-tuple-element.8.refs_0_, bf16[12,320]{1,0:T(8,128)(2,1)} %get-tuple-element.9.refs_1_, bf16[1,320,1024]{2,1,0:T(8,128)(2,1)} %get-tuple-element.10.refs_2_, ...), custom_call_target="tpu_custom_call" | custom-call | tf_op jit(solution)/shard_map/pallas_call | solution.py:470
